TPU v7x, 32 devices: a whole 2x2x4 slice. The times are simulated.
32 devices in a mesh: groups: 2 (over y), wide: 4 (over x, core), narrow: 4 (over z).
Axes of the slice: x: 2, y: 2, z: 4, core: 2. Of those that a mesh axis runs over, the one named last changes fastest.
Arguments:
- coords: bfloat16 [256, 3, 256], P(('groups', 'wide', 'narrow')), parts along dimension 0, may hold values from 0 to 1
- probe: float32 [256, 8, 256], P(('groups', 'wide', 'narrow')), parts along dimension 0
- kept: float32 [256, 8, 256], P(('groups', 'wide', 'narrow')), parts along dimension 0
- pairs: int32 [8, 4, 64, 2], P(('groups', 'wide'), 'narrow'), parts along dimension 0, may hold values from 0 to 11, as said below
- counts: int32 [8, 4], P(('groups', 'wide'), 'narrow'), parts along dimension 0, may hold values from 16 to 64, as said below
- send_list: int32 [8, 4, 4, 6], P(('groups', 'wide'), 'narrow'), parts along dimension 0, may hold values from 0 to 7
- target_list: int32 [8, 4, 4, 6], P(('groups', 'wide'), 'narrow'), parts along dimension 0, may hold values from 0 to 7
Outputs:
- next_block: float32 [256, 8, 256], P(('groups', 'wide', 'narrow')), parts along dimension 0
- projections: float32 [32, 8], P('groups'), parts along dimension 0
There are 2 independent parts, one for each index of `groups`. A program takes and returns all parts, laid end to end along the dimension named above; each array names one. Nothing has to cross between parts.
Inputs may be any that keep to these rules, and one draw needn't show every extreme that they name: The pairs of one device are distinct; column slots lie in 0 to 11, row blocks in 0 to 7. `counts`: some device has 64 live pairs.
All inputs are finite; a program needn't handle non-finite values.
Results may differ from a plain program's by a relative error of at most 0.0038.
Values may be sent and summed in bfloat16 or wider, within the bound.
A program may use at most 64 MiB of HBM per device.

v0:
```python
import functools

import jax
import jax.numpy as jnp
from jax import lax
from jax.experimental import pallas as pl
from jax.experimental.pallas import tpu as pltpu
from jax.sharding import PartitionSpec as P

MESH = pl.DeviceIdType.MESH

HALO = 2
TURN = 4
rho = 0.35
nugget = 1.0
eps = 1e-06

NT = (((1,), (1,)), ((), ()))
NN = (((1,), (0,)), ((), ()))


def split3(x):
    high = x.astype(jnp.bfloat16).astype(jnp.float32)
    rest = x - high
    mid = rest.astype(jnp.bfloat16).astype(jnp.float32)
    return high, mid, rest - mid


def norm_parts(sites):
    squared = jnp.sum(sites * sites, axis=0, keepdims=True) * (1.0 / rho**2)
    return split3(jnp.broadcast_to(squared, sites.shape))


def row_features(sites):
    high, mid, low = norm_parts(sites)
    place = lax.broadcasted_iota(jnp.int32, sites.shape, 0)
    tail = jnp.where(place < 3, 1.0, jnp.where(place == 3, high, jnp.where(place == 4, mid, low)))
    tail = jnp.where(place < 6, tail, 0.0)
    return jnp.concatenate([sites, sites, sites, tail], axis=0).astype(jnp.bfloat16)


def col_features(sites):
    high, mid, low = norm_parts(sites)
    place = lax.broadcasted_iota(jnp.int32, sites.shape, 0)
    tail = jnp.where(place == 0, high, jnp.where(place == 1, mid, jnp.where(place == 2, low, 1.0)))
    tail = jnp.where(place < 6, tail, 0.0)
    parts = split3(sites * (-2.0 / rho**2))
    return jnp.concatenate([*parts, tail], axis=0).T.astype(jnp.bfloat16)


def covariance(col_feat, row_feat):
    scaled2 = lax.dot_general(col_feat, row_feat, NN, preferred_element_type=jnp.float32)
    scaled2 = jnp.maximum(scaled2, 1e-12)
    support = jnp.maximum(1.0 - scaled2 * lax.rsqrt(scaled2), 0.0)
    square = support * support
    return (square * square * (1.25 - support)).astype(jnp.bfloat16)


def body(
    nw, nn,
    coords_ref, probe_ref, kept_ref, pairs_ref, counts_ref, send_ref, target_ref,
    next_ref, proj_ref,
    own, halo, stage, far, row_feat, col_feat, twice, masks, acc, split, part_w, part_n,
    halo_send, halo_recv, far_send, far_recv, pw_send, pw_recv, pn_send, pn_recv,
):
    w = lax.axis_index("wide")
    n = lax.axis_index("narrow")
    nb, probes, bs = probe_ref.shape
    basis = probes + kept_ref.shape[1]
    slots = send_ref.shape[3]
    pair_max = pairs_ref.shape[2]
    total_sites = float(nb * bs * nw * nn)

    barrier = pltpu.get_barrier_semaphore()
    for k in range(1, nw):
        pl.semaphore_signal(barrier, inc=1, device_id={"wide": lax.rem(w + k, nw)}, device_id_type=MESH)
    for k in range(1, nn):
        pl.semaphore_signal(barrier, inc=1, device_id={"narrow": lax.rem(n + k, nn)}, device_id_type=MESH)

    for b in range(nb):
        sites = jnp.concatenate(
            [coords_ref[b].astype(jnp.float32), jnp.zeros((8 - coords_ref.shape[1], bs), jnp.float32)], axis=0
        )
        own[b] = jnp.concatenate([sites, probe_ref[b]], axis=0).astype(jnp.bfloat16)

    for k in range(nw):
        w2 = lax.rem(w + k, nw)
        for s in range(slots):
            block = own[send_ref[0, 0, w2, s]]
            if k == 0:
                far[s] = block
            else:
                stage[k - 1, s] = block

    pl.semaphore_wait(barrier, nw + nn - 2)

    def far_copy(k):
        return pltpu.make_async_remote_copy(
            src_ref=stage.at[k - 1], dst_ref=far.at[pl.ds(k * slots, slots)],
            send_sem=far_send.at[k - 1], recv_sem=far_recv.at[k - 1],
            device_id={"wide": lax.rem(w + k, nw)}, device_id_type=MESH,
        )

    def up_copy():
        return pltpu.make_async_remote_copy(
            src_ref=own.at[pl.ds(nb - HALO, HALO)], dst_ref=halo.at[pl.ds(0, HALO)],
            send_sem=halo_send.at[0], recv_sem=halo_recv.at[0],
            device_id={"narrow": jnp.minimum(n + 1, nn - 1)}, device_id_type=MESH,
        )

    def down_copy():
        return pltpu.make_async_remote_copy(
            src_ref=own.at[pl.ds(0, HALO)], dst_ref=halo.at[pl.ds(HALO, HALO)],
            send_sem=halo_send.at[1], recv_sem=halo_recv.at[1],
            device_id={"narrow": jnp.maximum(n - 1, 0)}, device_id_type=MESH,
        )

    @pl.when(n < nn - 1)
    def _():
        up_copy().start()

    @pl.when(n > 0)
    def _():
        down_copy().start()

    for k in range(1, nw):
        far_copy(k).start()

    @pl.when(n == 0)
    def _():
        halo[0:HALO] = jnp.zeros((HALO,) + halo.shape[1:], halo.dtype)

    @pl.when(n == nn - 1)
    def _():
        halo[HALO:] = jnp.zeros((HALO,) + halo.shape[1:], halo.dtype)

    gram = jnp.zeros((3 * basis, basis), jnp.float32)
    for b in range(nb):
        parts = split3(jnp.concatenate([probe_ref[b], kept_ref[b]], axis=0))
        parts = [part.astype(jnp.bfloat16) for part in parts]
        stacked = jnp.concatenate(parts, axis=0)
        split[b] = stacked
        for part in parts:
            gram += lax.dot_general(stacked, part, NT, preferred_element_type=jnp.float32)
    gram = gram[2 * basis:] + gram[basis:2 * basis] + gram[:basis]

    mask_row = lax.broadcasted_iota(jnp.int32, (nb * probes, bs), 0) // probes
    for a in range(nb + 1):
        masks[a] = jnp.where(mask_row == a, 1.0, 0.0).astype(jnp.bfloat16)

    def prepare(slot, block):
        packed = block.astype(jnp.float32)
        col_feat[slot] = col_features(packed[:8])
        twice[slot] = jnp.concatenate([packed[8:], packed[8:]], axis=0).astype(jnp.bfloat16)
        return packed[:8]

    for b in range(nb):
        row_feat[b] = row_features(prepare(HALO + b, own[b]))

    acc[...] = nugget * probe_ref[...].reshape(nb * probes, bs)

    @pl.when(n > 0)
    def _():
        up_copy().wait_recv()

    @pl.when(n < nn - 1)
    def _():
        down_copy().wait_recv()

    for h in range(HALO):
        prepare(h, halo[h])
        prepare(HALO + nb + h, halo[HALO + h])

    def left(mask, probe2):
        return (mask.reshape(-1, 16, bs) * probe2[None]).reshape(mask.shape)

    count = counts_ref[0, 0]

    def local_turn(turn, carry):
        lefts, tiles = [], []
        for u in range(TURN):
            p = turn * TURN + u
            row = pairs_ref[0, 0, p, 0]
            slot = pairs_ref[0, 0, p, 1]
            within = n * nb - HALO + slot
            live = (p < count) & (within >= 0) & (within < nn * nb)
            lefts.append(left(masks[jnp.where(live, row, nb)], twice[slot]))
            tiles.append(covariance(col_feat[slot], row_feat[row]))
        acc[...] += lax.dot_general(
            jnp.concatenate(lefts, axis=1), jnp.concatenate(tiles, axis=0), NN,
            preferred_element_type=jnp.float32,
        )
        return carry

    lax.fori_loop(0, pair_max // TURN, local_turn, 0)

    for k in range(1, nw):
        far_copy(k).wait_recv()

    def far_turn(turn, carry):
        lefts, tiles = [], []
        for u in range(TURN):
            p = turn * TURN + u
            row = target_ref[0, 0, lax.rem(w - p // slots + nw, nw), p % slots]
            packed = far[p].astype(jnp.float32)
            probe2 = jnp.concatenate([packed[8:], packed[8:]], axis=0).astype(jnp.bfloat16)
            lefts.append(left(masks[row], probe2))
            tiles.append(covariance(col_features(packed[:8]), row_feat[row]))
        acc[...] += lax.dot_general(
            jnp.concatenate(lefts, axis=1), jnp.concatenate(tiles, axis=0), NN,
            preferred_element_type=jnp.float32,
        )
        return carry

    lax.fori_loop(0, nw * slots // TURN, far_turn, 0)

    inner = jnp.zeros((4 * probes, 4 * probes), jnp.float32)
    nothing = jnp.zeros((probes, bs), jnp.float32)
    for b in range(nb):
        high, mid, low = split3(acc[b * probes:(b + 1) * probes])
        first = jnp.concatenate([high, mid], axis=0).astype(jnp.bfloat16)
        second = jnp.concatenate([low, nothing], axis=0).astype(jnp.bfloat16)
        lhs = jnp.concatenate([first, second], axis=0)
        for u, part in enumerate((high, mid, low)):
            rhs = jnp.concatenate(
                [split[b, u * basis:(u + 1) * basis],
                 jnp.concatenate([part, nothing], axis=0).astype(jnp.bfloat16)], axis=0
            )
            inner += lax.dot_general(lhs, rhs, NT, preferred_element_type=jnp.float32)
    inner = inner[2 * probes:3 * probes] + inner[probes:2 * probes] + inner[:probes]
    inner = jnp.concatenate([inner, jnp.zeros((probes, 128 - inner.shape[1]), jnp.float32)], axis=1)
    gram = jnp.concatenate([gram, jnp.zeros((basis, 128 - basis), jnp.float32)], axis=1)

    def reduce(buf, axis, me, count, send, recv, value):
        buf[me] = value
        for k in range(1, count):
            pltpu.make_async_remote_copy(
                src_ref=buf.at[me], dst_ref=buf.at[me], send_sem=send.at[k - 1], recv_sem=recv.at[me],
                device_id={axis: lax.rem(me + k, count)}, device_id_type=MESH,
            ).start()
        for k in range(1, count):
            src = lax.rem(me + k, count)
            pltpu.make_async_remote_copy(
                src_ref=buf.at[src], dst_ref=buf.at[src], send_sem=send.at[k - 1], recv_sem=recv.at[src],
                device_id={axis: src}, device_id_type=MESH,
            ).wait_recv()
        total = buf[0]
        for k in range(1, count):
            total = total + buf[k]
        return total

    value = jnp.concatenate([inner, gram], axis=0)
    value = reduce(part_w, "wide", w, nw, pw_send, pw_recv, value)
    value = reduce(part_n, "narrow", n, nn, pn_send, pn_recv, value)

    raw = value[:probes]
    coef = raw * (1.0 / total_sites)
    lane = lax.broadcasted_iota(jnp.int32, raw.shape, 1)
    line = lax.broadcasted_iota(jnp.int32, raw.shape, 0)
    norm = jnp.sum(jnp.where(lane == line + basis, raw, 0.0), axis=1, keepdims=True)
    columns = [jnp.sum(jnp.where(lane == j, coef, 0.0), axis=1, keepdims=True) for j in range(basis)]
    coupled = jnp.zeros_like(raw)
    for j in range(basis):
        coupled = coupled + columns[j] * value[probes + j:probes + j + 1]
    quad = jnp.sum(jnp.where(lane < basis, coef * (coupled - 2.0 * raw), 0.0), axis=1, keepdims=True)
    power = jnp.maximum((norm + quad) * (1.0 / total_sites), 0.0)
    inv = 1.0 / jnp.sqrt(power + eps)
    proj_ref[...] = jnp.concatenate([coef] * (128 // probes), axis=0).T[:basis, :probes]
    for b in range(nb):
        fresh = acc[b * probes:(b + 1) * probes]
        for j in range(basis):
            source = probe_ref[b, j:j + 1] if j < probes else kept_ref[b, j - probes:j - probes + 1]
            fresh = fresh - columns[j] * source
        next_ref[b] = fresh * inv

    @pl.when(n < nn - 1)
    def _():
        up_copy().wait_send()

    @pl.when(n > 0)
    def _():
        down_copy().wait_send()

    for k in range(1, nw):
        far_copy(k).wait_send()
    for buf, axis, me, cnt, send, recv in (
        (part_w, "wide", w, nw, pw_send, pw_recv), (part_n, "narrow", n, nn, pn_send, pn_recv)
    ):
        for k in range(1, cnt):
            pltpu.make_async_remote_copy(
                src_ref=buf.at[me], dst_ref=buf.at[me], send_sem=send.at[k - 1], recv_sem=recv.at[me],
                device_id={axis: lax.rem(me + k, cnt)}, device_id_type=MESH,
            ).wait_send()


def solution(mesh):
    nw, nn = mesh.shape["wide"], mesh.shape["narrow"]

    def shards(coords, probe, kept, pairs, counts, send_list, target_list):
        nb, probes, bs = probe.shape
        basis = probes + kept.shape[1]
        slots = send_list.shape[3]
        bf16, f32 = jnp.bfloat16, jnp.float32
        vmem = pl.BlockSpec(memory_space=pltpu.VMEM)
        smem = pl.BlockSpec(memory_space=pltpu.SMEM)
        dma = pltpu.SemaphoreType.DMA
        return pl.pallas_call(
            functools.partial(body, nw, nn),
            out_shape=(
                jax.ShapeDtypeStruct((nb, probes, bs), f32),
                jax.ShapeDtypeStruct((basis, probes), f32),
            ),
            in_specs=[vmem] * 3 + [smem] * 4,
            out_specs=(vmem, vmem),
            scratch_shapes=[
                pltpu.VMEM((nb, 16, bs), bf16),
                pltpu.VMEM((2 * HALO, 16, bs), bf16),
                pltpu.VMEM((nw - 1, slots, 16, bs), bf16),
                pltpu.VMEM((nw * slots, 16, bs), bf16),
                pltpu.VMEM((nb, 32, bs), bf16),
                pltpu.VMEM((nb + 2 * HALO, bs, 32), bf16),
                pltpu.VMEM((nb + 2 * HALO, 16, bs), bf16),
                pltpu.VMEM((nb + 1, nb * probes, bs), bf16),
                pltpu.VMEM((nb * probes, bs), f32),
                pltpu.VMEM((nb, 3 * basis, bs), bf16),
                pltpu.VMEM((nw, probes + basis, 128), f32),
                pltpu.VMEM((nn, probes + basis, 128), f32),
                dma((2,)), dma((2,)),
                dma((nw - 1,)), dma((nw - 1,)),
                dma((nw - 1,)), dma((nw,)),
                dma((nn - 1,)), dma((nn,)),
            ],
            compiler_params=pltpu.CompilerParams(
                collective_id=0, has_side_effects=True, vmem_limit_bytes=32 * 2**20
            ),
            name="lanczos_step",
        )(coords, probe, kept, pairs, counts, send_list, target_list)

    blocks = P(("groups", "wide", "narrow"), None, None)
    lists = P(("groups", "wide"), "narrow", None, None)
    in_specs = (blocks, blocks, blocks, lists, P(("groups", "wide"), "narrow"), lists, lists)
    out_specs = (blocks, P("groups", None))
    return jax.shard_map(shards, mesh=mesh, in_specs=in_specs, out_specs=out_specs, check_vma=False)
```

profile of v0, /device:TPU:0, one launch (start us, length us, event | category | flops | bytes accessed | tf_op | source)
XLA Modules:
  0.0 36.0 jit_solution(6266144387437220265)
XLA Ops:
  1.3 0.0 copy-start.4
  1.3 0.7 %copy.9.coords_ref = bf16[8,3,256]{2,1,0:T(4,128)(2,1)S(1)} copy(bf16[8,3,256]{2,0,1:T(8,128)(2,1)} %param.7) | data formatting | bytes 24576 | tf_op args[0]
  2.0 0.0 copy-done.4
  2.0 0.0 copy-start.2
  2.0 0.0 copy-start.3
  2.0 0.1 copy.10.pairs_ref
  2.1 0.6 %copy-done.2 = s32[1,1,4,6]{3,2,1,0:T(4,128)S(1)} copy-done((s32[1,1,4,6]{3,2,1,0:T(4,128)S(1)}, s32[1,1,4,6]{3,2,1,0:T(4,128)}, u32[]{:S(2)}) %copy-start.2) | copy-done | bytes 120
  2.7 0.0 copy-done.3
  2.7 0.0 copy-start
  2.7 0.8 %copy-done = f32[8,8,256]{2,1,0:T(8,128)S(1)} copy-done((f32[8,8,256]{2,1,0:T(8,128)S(1)}, f32[8,8,256]{2,1,0:T(8,128)}, u32[]{:S(2)}) %copy-start) | copy-done | bytes 65560
  3.6 0.0 copy-start.1
  3.6 0.8 %copy-done.1 = f32[8,8,256]{2,1,0:T(8,128)S(1)} copy-done((f32[8,8,256]{2,1,0:T(8,128)S(1)}, f32[8,8,256]{2,1,0:T(8,128)}, u32[]{:S(2)}) %copy-start.1) | copy-done | bytes 65560
  4.4 30.3 %lanczos_step.1 = (f32[8,8,256]{2,1,0:T(8,128)S(1)}, f32[16,8]{1,0:T(8,128)S(1)}) custom-call(bf16[8,3,256]{2,1,0:T(4,128)(2,1)S(1)} %copy.9.coords_ref, f32[8,8,256]{2,1,0:T(8,128)S(1)} %copy-done, f32[8,8,256]{2,1,0:T(8,128)S(1)} %copy-done.1, s32[1,1,64,2]{3,2,1,0:T(8,128)S(1)} %copy.10.pairs_ref, s32[1,1]{1,0:T(1,128)S(6)} %copy.13.counts_ref, ...), custom_call_target="tpu_custom_call" | custom-call | tf_op jit(solution)/shard_map/lanczos_step/pallas_call | solution.py:307
  34.7 0.7 %copy.11 = f32[16,8]{0,1:T(8,128)} copy(f32[16,8]{1,0:T(8,128)S(1)} %get-tuple-element.3) | data formatting | bytes 1024 | tf_op jit(solution)/shard_map/lanczos_step/pallas_call | solution.py:307
  35.4 0.6 %copy.14 = f32[8,8,256]{2,1,0:T(8,128)} copy(f32[8,8,256]{2,1,0:T(8,128)S(1)} %get-tuple-element.6) | data formatting | bytes 131072
Async XLA Ops:
  1.3 0.7 %copy-start.4 = (s32[1,1,64,2]{2,3,1,0:T(2,128)S(1)}, s32[1,1,64,2]{2,3,1,0:T(2,128)}, u32[]{:S(2)}) copy-start(s32[1,1,64,2]{2,3,1,0:T(2,128)} %param.10) | copy-start | bytes 1540
  2.0 0.7 %copy-start.2 = (s32[1,1,4,6]{3,2,1,0:T(4,128)S(1)}, s32[1,1,4,6]{3,2,1,0:T(4,128)}, u32[]{:S(2)}) copy-start(s32[1,1,4,6]{3,2,1,0:T(4,128)} %send_ref.1) | copy-start | bytes 292
  2.0 0.7 %copy-start.3 = (s32[1,1,4,6]{3,2,1,0:T(4,128)S(1)}, s32[1,1,4,6]{3,2,1,0:T(4,128)}, u32[]{:S(2)}) copy-start(s32[1,1,4,6]{3,2,1,0:T(4,128)} %target_ref.1) | copy-start | bytes 292
  2.7 0.8 %copy-start = (f32[8,8,256]{2,1,0:T(8,128)S(1)}, f32[8,8,256]{2,1,0:T(8,128)}, u32[]{:S(2)}) copy-start(f32[8,8,256]{2,1,0:T(8,128)} %probe_ref.1) | copy-start | bytes 196612
  3.6 0.8 %copy-start.1 = (f32[8,8,256]{2,1,0:T(8,128)S(1)}, f32[8,8,256]{2,1,0:T(8,128)}, u32[]{:S(2)}) copy-start(f32[8,8,256]{2,1,0:T(8,128)} %kept_ref.1) | copy-start | bytes 196612
where the time goes:
time: 36.3 us; the launch traced here: 36 us
  Pallas kernels  30.3 us (83%)
  local copies, waits for them, and re-layouts  4.38 us (12%)
  between operations  1.32 us (4%)
    pallas_call x1, Pallas kernels, shards(): pl.pallas_call(functools.partial(body, nw, nn), out_shape=(jax.ShapeDtype...  30.3 us
    unnamed x13, local copies, waits for them, and re-layouts  3.71 us

commit v1 on v0

--- a/solution.py
+++ b/solution.py
@@ -10,7 +10,7 @@
 MESH = pl.DeviceIdType.MESH
 
 HALO = 2
-TURN = 4
+TURN = 16
 rho = 0.35
 nugget = 1.0
 eps = 1e-06
@@ -58,8 +58,9 @@
 
 def body(
     nw, nn,
-    coords_ref, probe_ref, kept_ref, pairs_ref, counts_ref, send_ref, target_ref,
+    coords_hbm, probe_hbm, kept_hbm, pairs_hbm, counts_hbm, send_hbm, target_hbm,
     next_ref, proj_ref,
+    coords_ref, probe_ref, kept_ref, pairs_ref, counts_ref, send_ref, target_ref, in_sem,
     own, halo, stage, far, row_feat, col_feat, twice, masks, acc, split, part_w, part_n,
     halo_send, halo_recv, far_send, far_recv, pw_send, pw_recv, pn_send, pn_recv,
 ):
@@ -68,8 +69,18 @@
     nb, probes, bs = probe_ref.shape
     basis = probes + kept_ref.shape[1]
     slots = send_ref.shape[3]
-    pair_max = pairs_ref.shape[2]
+    pair_max = pairs_ref.shape[3]
     total_sites = float(nb * bs * nw * nn)
+
+    inputs = [
+        pltpu.make_async_copy(src, dst, in_sem.at[place])
+        for place, (src, dst) in enumerate((
+            (coords_hbm, coords_ref), (probe_hbm, probe_ref), (send_hbm, send_ref), (kept_hbm, kept_ref),
+            (target_hbm, target_ref), (pairs_hbm, pairs_ref), (counts_hbm, counts_ref),
+        ))
+    ]
+    for copy in inputs:
+        copy.start()
 
     barrier = pltpu.get_barrier_semaphore()
     for k in range(1, nw):
@@ -77,10 +88,14 @@
     for k in range(1, nn):
         pl.semaphore_signal(barrier, inc=1, device_id={"narrow": lax.rem(n + k, nn)}, device_id_type=MESH)
 
-    for b in range(nb):
-        sites = jnp.concatenate(
-            [coords_ref[b].astype(jnp.float32), jnp.zeros((8 - coords_ref.shape[1], bs), jnp.float32)], axis=0
-        )
+    for copy in inputs[:3]:
+        copy.wait()
+    sites_all = coords_ref[...].astype(jnp.float32)
+    site_line = lax.broadcasted_iota(jnp.int32, (8, bs), 0)
+    for b in range(nb):
+        sites = jnp.zeros((8, bs), jnp.float32)
+        for component in range(sites_all.shape[0]):
+            sites = jnp.where(site_line == component, sites_all[component, b:b + 1], sites)
         own[b] = jnp.concatenate([sites, probe_ref[b]], axis=0).astype(jnp.bfloat16)
 
     for k in range(nw):
@@ -134,19 +149,22 @@
     def _():
         halo[HALO:] = jnp.zeros((HALO,) + halo.shape[1:], halo.dtype)
 
-    gram = jnp.zeros((3 * basis, basis), jnp.float32)
-    for b in range(nb):
-        parts = split3(jnp.concatenate([probe_ref[b], kept_ref[b]], axis=0))
-        parts = [part.astype(jnp.bfloat16) for part in parts]
-        stacked = jnp.concatenate(parts, axis=0)
-        split[b] = stacked
-        for part in parts:
-            gram += lax.dot_general(stacked, part, NT, preferred_element_type=jnp.float32)
-    gram = gram[2 * basis:] + gram[basis:2 * basis] + gram[:basis]
-
     mask_row = lax.broadcasted_iota(jnp.int32, (nb * probes, bs), 0) // probes
     for a in range(nb + 1):
         masks[a] = jnp.where(mask_row == a, 1.0, 0.0).astype(jnp.bfloat16)
+
+    for copy in inputs[3:]:
+        copy.wait()
+    for b in range(nb):
+        parts = split3(jnp.concatenate([probe_ref[b], kept_ref[b]], axis=0))
+        stacked = jnp.concatenate([part.astype(jnp.bfloat16) for part in parts], axis=0)
+        split[:, b * bs:(b + 1) * bs] = stacked
+    gram = jnp.zeros((3 * basis, basis), jnp.float32)
+    for u in range(3):
+        gram += lax.dot_general(
+            split[...], split[u * basis:(u + 1) * basis], NT, preferred_element_type=jnp.float32
+        )
+    gram = gram[2 * basis:] + gram[basis:2 * basis] + gram[:basis]
 
     def prepare(slot, block):
         packed = block.astype(jnp.float32)
@@ -159,48 +177,13 @@
 
     acc[...] = nugget * probe_ref[...].reshape(nb * probes, bs)
 
-    @pl.when(n > 0)
-    def _():
-        up_copy().wait_recv()
-
-    @pl.when(n < nn - 1)
-    def _():
-        down_copy().wait_recv()
-
-    for h in range(HALO):
-        prepare(h, halo[h])
-        prepare(HALO + nb + h, halo[HALO + h])
-
     def left(mask, probe2):
         return (mask.reshape(-1, 16, bs) * probe2[None]).reshape(mask.shape)
 
-    count = counts_ref[0, 0]
-
-    def local_turn(turn, carry):
+    def far_turn(first, size):
         lefts, tiles = [], []
-        for u in range(TURN):
-            p = turn * TURN + u
-            row = pairs_ref[0, 0, p, 0]
-            slot = pairs_ref[0, 0, p, 1]
-            within = n * nb - HALO + slot
-            live = (p < count) & (within >= 0) & (within < nn * nb)
-            lefts.append(left(masks[jnp.where(live, row, nb)], twice[slot]))
-            tiles.append(covariance(col_feat[slot], row_feat[row]))
-        acc[...] += lax.dot_general(
-            jnp.concatenate(lefts, axis=1), jnp.concatenate(tiles, axis=0), NN,
-            preferred_element_type=jnp.float32,
-        )
-        return carry
-
-    lax.fori_loop(0, pair_max // TURN, local_turn, 0)
-
-    for k in range(1, nw):
-        far_copy(k).wait_recv()
-
-    def far_turn(turn, carry):
-        lefts, tiles = [], []
-        for u in range(TURN):
-            p = turn * TURN + u
+        for u in range(size):
+            p = first + u
             row = target_ref[0, 0, lax.rem(w - p // slots + nw, nw), p % slots]
             packed = far[p].astype(jnp.float32)
             probe2 = jnp.concatenate([packed[8:], packed[8:]], axis=0).astype(jnp.bfloat16)
@@ -210,23 +193,66 @@
             jnp.concatenate(lefts, axis=1), jnp.concatenate(tiles, axis=0), NN,
             preferred_element_type=jnp.float32,
         )
+
+    far_turn(0, slots)
+
+    @pl.when(n > 0)
+    def _():
+        up_copy().wait_recv()
+
+    @pl.when(n < nn - 1)
+    def _():
+        down_copy().wait_recv()
+
+    for h in range(HALO):
+        prepare(h, halo[h])
+        prepare(HALO + nb + h, halo[HALO + h])
+
+    count = counts_ref[0, 0]
+
+    def local_turn(turn, carry):
+        lefts, tiles = [], []
+        for u in range(TURN):
+            p = turn * TURN + u
+            row = pairs_ref[0, 0, 0, p]
+            slot = pairs_ref[0, 0, 1, p]
+            within = n * nb - HALO + slot
+            live = (p < count) & (within >= 0) & (within < nn * nb)
+            lefts.append(left(masks[jnp.where(live, row, nb)], twice[slot]))
+            tiles.append(covariance(col_feat[slot], row_feat[row]))
+        acc[...] += lax.dot_general(
+            jnp.concatenate(lefts, axis=1), jnp.concatenate(tiles, axis=0), NN,
+            preferred_element_type=jnp.float32,
+        )
         return carry
 
-    lax.fori_loop(0, nw * slots // TURN, far_turn, 0)
-
-    inner = jnp.zeros((4 * probes, 4 * probes), jnp.float32)
+    lax.fori_loop(0, pair_max // TURN, local_turn, 0)
+
+    for k in range(1, nw):
+        far_copy(k).wait_recv()
+
+    def far_source(source, carry):
+        far_turn(source * slots, slots)
+        return carry
+
+    lax.fori_loop(1, nw, far_source, 0)
+
     nothing = jnp.zeros((probes, bs), jnp.float32)
+    lhs, rhs = [], [[], [], []]
     for b in range(nb):
         high, mid, low = split3(acc[b * probes:(b + 1) * probes])
         first = jnp.concatenate([high, mid], axis=0).astype(jnp.bfloat16)
         second = jnp.concatenate([low, nothing], axis=0).astype(jnp.bfloat16)
-        lhs = jnp.concatenate([first, second], axis=0)
+        lhs.append(jnp.concatenate([first, second], axis=0))
         for u, part in enumerate((high, mid, low)):
-            rhs = jnp.concatenate(
-                [split[b, u * basis:(u + 1) * basis],
-                 jnp.concatenate([part, nothing], axis=0).astype(jnp.bfloat16)], axis=0
-            )
-            inner += lax.dot_general(lhs, rhs, NT, preferred_element_type=jnp.float32)
+            rhs[u].append(jnp.concatenate([part, nothing], axis=0).astype(jnp.bfloat16))
+    lhs = jnp.concatenate(lhs, axis=1)
+    inner = jnp.zeros((4 * probes, 4 * probes), jnp.float32)
+    for u in range(3):
+        both = jnp.concatenate(
+            [split[u * basis:(u + 1) * basis], jnp.concatenate(rhs[u], axis=1)], axis=0
+        )
+        inner += lax.dot_general(lhs, both, NT, preferred_element_type=jnp.float32)
     inner = inner[2 * probes:3 * probes] + inner[probes:2 * probes] + inner[:probes]
     inner = jnp.concatenate([inner, jnp.zeros((probes, 128 - inner.shape[1]), jnp.float32)], axis=1)
     gram = jnp.concatenate([gram, jnp.zeros((basis, 128 - basis), jnp.float32)], axis=1)
@@ -265,7 +291,7 @@
     quad = jnp.sum(jnp.where(lane < basis, coef * (coupled - 2.0 * raw), 0.0), axis=1, keepdims=True)
     power = jnp.maximum((norm + quad) * (1.0 / total_sites), 0.0)
     inv = 1.0 / jnp.sqrt(power + eps)
-    proj_ref[...] = jnp.concatenate([coef] * (128 // probes), axis=0).T[:basis, :probes]
+    proj_ref[...] = coef[:, :basis]
     for b in range(nb):
         fresh = acc[b * probes:(b + 1) * probes]
         for j in range(basis):
@@ -302,17 +328,24 @@
         slots = send_list.shape[3]
         bf16, f32 = jnp.bfloat16, jnp.float32
         vmem = pl.BlockSpec(memory_space=pltpu.VMEM)
-        smem = pl.BlockSpec(memory_space=pltpu.SMEM)
         dma = pltpu.SemaphoreType.DMA
-        return pl.pallas_call(
+        next_block, coupled = pl.pallas_call(
             functools.partial(body, nw, nn),
             out_shape=(
                 jax.ShapeDtypeStruct((nb, probes, bs), f32),
-                jax.ShapeDtypeStruct((basis, probes), f32),
+                jax.ShapeDtypeStruct((probes, basis), f32),
             ),
-            in_specs=[vmem] * 3 + [smem] * 4,
+            in_specs=[pl.BlockSpec(memory_space=pl.ANY)] * 7,
             out_specs=(vmem, vmem),
             scratch_shapes=[
+                pltpu.VMEM((coords.shape[1], nb, bs), bf16),
+                pltpu.VMEM(probe.shape, f32),
+                pltpu.VMEM(kept.shape, f32),
+                pltpu.SMEM((1, 1, 2, pairs.shape[2]), jnp.int32),
+                pltpu.SMEM(counts.shape, jnp.int32),
+                pltpu.SMEM(send_list.shape, jnp.int32),
+                pltpu.SMEM(target_list.shape, jnp.int32),
+                dma((7,)),
                 pltpu.VMEM((nb, 16, bs), bf16),
                 pltpu.VMEM((2 * HALO, 16, bs), bf16),
                 pltpu.VMEM((nw - 1, slots, 16, bs), bf16),
@@ -322,7 +355,7 @@
                 pltpu.VMEM((nb + 2 * HALO, 16, bs), bf16),
                 pltpu.VMEM((nb + 1, nb * probes, bs), bf16),
                 pltpu.VMEM((nb * probes, bs), f32),
-                pltpu.VMEM((nb, 3 * basis, bs), bf16),
+                pltpu.VMEM((3 * basis, nb * bs), bf16),
                 pltpu.VMEM((nw, probes + basis, 128), f32),
                 pltpu.VMEM((nn, probes + basis, 128), f32),
                 dma((2,)), dma((2,)),
@@ -331,10 +364,13 @@
                 dma((nn - 1,)), dma((nn,)),
             ],
             compiler_params=pltpu.CompilerParams(
-                collective_id=0, has_side_effects=True, vmem_limit_bytes=32 * 2**20
+                collective_id=0, has_side_effects=True, vmem_limit_bytes=56 * 2**20
             ),
             name="lanczos_step",
-        )(coords, probe, kept, pairs, counts, send_list, target_list)
+        )(
+            coords.transpose(1, 0, 2), probe, kept, pairs.transpose(0, 1, 3, 2), counts, send_list, target_list
+        )
+        return next_block, coupled.T
 
     blocks = P(("groups", "wide", "narrow"), None, None)
     lists = P(("groups", "wide"), "narrow", None, None)

time: 36.3 us -> 28.9 us (0.80)
  Pallas kernels: 30.3 us -> 25.3 us
  local copies, waits for them, and re-layouts: 4.38 us -> 2.07 us
    pallas_call x1, Pallas kernels: 30.3 us -> 25.3 us  [shards(): pl.pallas_call(functools.partial(body, nw, nn), out_shape=(jax.ShapeDtype...]
    unnamed x13 -> x4, local copies, waits for them, and re-layouts: 3.71 us -> 2.07 us
    pallas_call x1 -> x0, local copies, waits for them, and re-layouts: 0.66 us -> none  [shards(): pl.pallas_call(functools.partial(body, nw, nn), out_shape=(jax.ShapeDtype...]
where the time goes in v1:
time: 28.9 us; the launch traced here: 28.7 us
  Pallas kernels  25.3 us (88%)
  local copies, waits for them, and re-layouts  2.07 us (7%)
  between operations  1.29 us (4%)
    pallas_call x1, Pallas kernels, shards(): pl.pallas_call(functools.partial(body, nw, nn), out_shape=(jax.ShapeDtype...  25.3 us
    unnamed x4, local copies, waits for them, and re-layouts  2.07 us

profile of v1, /device:TPU:0, one launch (start us, length us, event | category | flops | bytes accessed | tf_op | source)
XLA Modules:
  0.0 28.7 jit_solution(7516562672131772444)
XLA Ops:
  1.3 25.3 %lanczos_step.1 = (f32[8,8,256]{2,1,0:T(8,128)}, f32[8,16]{1,0:T(8,128)}) custom-call(bf16[3,8,256]{2,1,0:T(8,128)(2,1)} %bitcast.3, f32[8,8,256]{2,1,0:T(8,128)} %probe_hbm.1, f32[8,8,256]{2,1,0:T(8,128)} %kept_hbm.1, s32[1,1,2,64]{3,2,1,0:T(2,128)} %bitcast.5, s32[1,1]{1,0:T(1,128)S(6)} %copy.11.counts_hbm, s32[1,1,4,6]{3,2,1,0:T(4,128)} %send_hbm.1, ...), custom_call_target="tpu_custom_call" | custom-call | tf_op jit(solution)/shard_map/lanczos_step/pallas_call | solution.py:332
  26.6 0.0 copy-start
  26.6 1.5 %copy.12 = f32[8,8,256]{2,1,0:T(8,128)} copy(f32[8,8,256]{2,1,0:T(8,128)} %get-tuple-element.8) | data formatting | bytes 131072
  28.1 0.0 copy-done
  28.1 0.6 %copy.13 = f32[16,8]{0,1:T(8,128)} copy(f32[16,8]{0,1:T(8,128)S(1)} %bitcast.4) | data formatting | bytes 1024
Async XLA Ops:
  26.6 1.5 %copy-start = (f32[8,16]{1,0:T(8,128)S(1)}, f32[8,16]{1,0:T(8,128)}, u32[]{:S(2)}) copy-start(f32[8,16]{1,0:T(8,128)} %get-tuple-element.5) | copy-start | bytes 1540

commit v2 on v1

--- a/solution.py
+++ b/solution.py
@@ -10,7 +10,7 @@
 MESH = pl.DeviceIdType.MESH
 
 HALO = 2
-TURN = 16
+TURN = 32
 rho = 0.35
 nugget = 1.0
 eps = 1e-06
@@ -61,8 +61,9 @@
     coords_hbm, probe_hbm, kept_hbm, pairs_hbm, counts_hbm, send_hbm, target_hbm,
     next_ref, proj_ref,
     coords_ref, probe_ref, kept_ref, pairs_ref, counts_ref, send_ref, target_ref, in_sem,
-    own, halo, stage, far, row_feat, col_feat, twice, masks, acc, split, part_w, part_n,
-    halo_send, halo_recv, far_send, far_recv, pw_send, pw_recv, pn_send, pn_recv,
+    own, halo, stage, far, row_feat, col_feat, twice, masks, acc, split, gram_w, gram_n, last_w, last_n, last_all,
+    halo_send, halo_recv, far_send, far_recv, gw_send, gw_recv, gn_send, gn_recv,
+    lw_send, lw_recv, ln_send, ln_recv, la_send, la_recv,
 ):
     w = lax.axis_index("wide")
     n = lax.axis_index("narrow")
@@ -71,6 +72,21 @@
     slots = send_ref.shape[3]
     pair_max = pairs_ref.shape[3]
     total_sites = float(nb * bs * nw * nn)
+
+    def along_wide(k):
+        return {"wide": lax.rem(w + k, nw)}
+
+    def along_narrow(k):
+        return {"narrow": lax.rem(n + k, nn)}
+
+    def along_both(k):
+        return {"wide": lax.rem(w + k // nn, nw), "narrow": lax.rem(n + k % nn, nn)}
+
+    direct = nw * nn <= 32
+    if direct:
+        partners = [along_both(k) for k in range(1, nw * nn)]
+    else:
+        partners = [along_wide(k) for k in range(1, nw)] + [along_narrow(k) for k in range(1, nn)]
 
     inputs = [
         pltpu.make_async_copy(src, dst, in_sem.at[place])
@@ -83,10 +99,20 @@
         copy.start()
 
     barrier = pltpu.get_barrier_semaphore()
-    for k in range(1, nw):
-        pl.semaphore_signal(barrier, inc=1, device_id={"wide": lax.rem(w + k, nw)}, device_id_type=MESH)
-    for k in range(1, nn):
-        pl.semaphore_signal(barrier, inc=1, device_id={"narrow": lax.rem(n + k, nn)}, device_id_type=MESH)
+    for device in partners:
+        pl.semaphore_signal(barrier, inc=1, device_id=device, device_id_type=MESH)
+
+    mask_row = lax.broadcasted_iota(jnp.int32, (nb * probes, bs), 0) // probes
+    for a in range(nb + 1):
+        masks[a] = jnp.where(mask_row == a, 1.0, 0.0).astype(jnp.bfloat16)
+
+    @pl.when(n == 0)
+    def _():
+        halo[0:HALO] = jnp.zeros((HALO,) + halo.shape[1:], halo.dtype)
+
+    @pl.when(n == nn - 1)
+    def _():
+        halo[HALO:] = jnp.zeros((HALO,) + halo.shape[1:], halo.dtype)
 
     for copy in inputs[:3]:
         copy.wait()
@@ -107,7 +133,7 @@
             else:
                 stage[k - 1, s] = block
 
-    pl.semaphore_wait(barrier, nw + nn - 2)
+    pl.semaphore_wait(barrier, len(partners))
 
     def far_copy(k):
         return pltpu.make_async_remote_copy(
@@ -141,17 +167,53 @@
     for k in range(1, nw):
         far_copy(k).start()
 
-    @pl.when(n == 0)
-    def _():
-        halo[0:HALO] = jnp.zeros((HALO,) + halo.shape[1:], halo.dtype)
-
-    @pl.when(n == nn - 1)
-    def _():
-        halo[HALO:] = jnp.zeros((HALO,) + halo.shape[1:], halo.dtype)
-
-    mask_row = lax.broadcasted_iota(jnp.int32, (nb * probes, bs), 0) // probes
-    for a in range(nb + 1):
-        masks[a] = jnp.where(mask_row == a, 1.0, 0.0).astype(jnp.bfloat16)
+    def exchange(buf, send, recv, device_of, me, count):
+        def copies():
+            return [
+                pltpu.make_async_remote_copy(
+                    src_ref=buf.at[me], dst_ref=buf.at[me], send_sem=send.at[k - 1], recv_sem=recv.at[me],
+                    device_id=device_of(k), device_id_type=MESH,
+                )
+                for k in range(1, count)
+            ]
+
+        def start(value):
+            buf[me] = value
+            for copy in copies():
+                copy.start()
+
+        def finish(source_of):
+            for k in range(1, count):
+                source = source_of(k)
+                pltpu.make_async_remote_copy(
+                    src_ref=buf.at[source], dst_ref=buf.at[source], send_sem=send.at[k - 1],
+                    recv_sem=recv.at[source], device_id=device_of(k), device_id_type=MESH,
+                ).wait_recv()
+            terms = [buf[k] for k in range(count)]
+            while len(terms) > 1:
+                terms = [sum(terms[k + 1:k + 2], terms[k]) for k in range(0, len(terms), 2)]
+            return terms[0]
+
+        def drain():
+            for copy in copies():
+                copy.wait_send()
+
+        return start, finish, drain
+
+    def wide_source(k):
+        return lax.rem(w + k, nw)
+
+    def narrow_source(k):
+        return lax.rem(n + k, nn)
+
+    def both_source(k):
+        return lax.rem(w + k // nn, nw) * nn + lax.rem(n + k % nn, nn)
+
+    gram_wide = exchange(gram_w, gw_send, gw_recv, along_wide, w, nw)
+    gram_narrow = exchange(gram_n, gn_send, gn_recv, along_narrow, n, nn)
+    last_wide = exchange(last_w, lw_send, lw_recv, along_wide, w, nw)
+    last_narrow = exchange(last_n, ln_send, ln_recv, along_narrow, n, nn)
+    last_both = exchange(last_all, la_send, la_recv, along_both, w * nn + n, nw * nn if direct else 1)
 
     for copy in inputs[3:]:
         copy.wait()
@@ -165,6 +227,7 @@
             split[...], split[u * basis:(u + 1) * basis], NT, preferred_element_type=jnp.float32
         )
     gram = gram[2 * basis:] + gram[basis:2 * basis] + gram[:basis]
+    gram_wide[0](jnp.concatenate([gram, jnp.zeros((basis, 128 - basis), jnp.float32)], axis=1))
 
     def prepare(slot, block):
         packed = block.astype(jnp.float32)
@@ -227,6 +290,7 @@
         return carry
 
     lax.fori_loop(0, pair_max // TURN, local_turn, 0)
+    gram_narrow[0](gram_wide[1](wide_source))
 
     for k in range(1, nw):
         far_copy(k).wait_recv()
@@ -235,7 +299,10 @@
         far_turn(source * slots, slots)
         return carry
 
-    lax.fori_loop(1, nw, far_source, 0)
+    if nw <= 4:
+        far_turn(slots, (nw - 1) * slots)
+    else:
+        lax.fori_loop(1, nw, far_source, 0)
 
     nothing = jnp.zeros((probes, bs), jnp.float32)
     lhs, rhs = [], [[], [], []]
@@ -255,31 +322,15 @@
         inner += lax.dot_general(lhs, both, NT, preferred_element_type=jnp.float32)
     inner = inner[2 * probes:3 * probes] + inner[probes:2 * probes] + inner[:probes]
     inner = jnp.concatenate([inner, jnp.zeros((probes, 128 - inner.shape[1]), jnp.float32)], axis=1)
-    gram = jnp.concatenate([gram, jnp.zeros((basis, 128 - basis), jnp.float32)], axis=1)
-
-    def reduce(buf, axis, me, count, send, recv, value):
-        buf[me] = value
-        for k in range(1, count):
-            pltpu.make_async_remote_copy(
-                src_ref=buf.at[me], dst_ref=buf.at[me], send_sem=send.at[k - 1], recv_sem=recv.at[me],
-                device_id={axis: lax.rem(me + k, count)}, device_id_type=MESH,
-            ).start()
-        for k in range(1, count):
-            src = lax.rem(me + k, count)
-            pltpu.make_async_remote_copy(
-                src_ref=buf.at[src], dst_ref=buf.at[src], send_sem=send.at[k - 1], recv_sem=recv.at[src],
-                device_id={axis: src}, device_id_type=MESH,
-            ).wait_recv()
-        total = buf[0]
-        for k in range(1, count):
-            total = total + buf[k]
-        return total
-
-    value = jnp.concatenate([inner, gram], axis=0)
-    value = reduce(part_w, "wide", w, nw, pw_send, pw_recv, value)
-    value = reduce(part_n, "narrow", n, nn, pn_send, pn_recv, value)
-
-    raw = value[:probes]
+    if direct:
+        last_both[0](inner)
+        gram = gram_narrow[1](narrow_source)
+        raw = last_both[1](both_source)
+    else:
+        last_wide[0](inner)
+        gram = gram_narrow[1](narrow_source)
+        last_narrow[0](last_wide[1](wide_source))
+        raw = last_narrow[1](narrow_source)
     coef = raw * (1.0 / total_sites)
     lane = lax.broadcasted_iota(jnp.int32, raw.shape, 1)
     line = lax.broadcasted_iota(jnp.int32, raw.shape, 0)
@@ -287,7 +338,7 @@
     columns = [jnp.sum(jnp.where(lane == j, coef, 0.0), axis=1, keepdims=True) for j in range(basis)]
     coupled = jnp.zeros_like(raw)
     for j in range(basis):
-        coupled = coupled + columns[j] * value[probes + j:probes + j + 1]
+        coupled = coupled + columns[j] * gram[j:j + 1]
     quad = jnp.sum(jnp.where(lane < basis, coef * (coupled - 2.0 * raw), 0.0), axis=1, keepdims=True)
     power = jnp.maximum((norm + quad) * (1.0 / total_sites), 0.0)
     inv = 1.0 / jnp.sqrt(power + eps)
@@ -309,14 +360,13 @@
 
     for k in range(1, nw):
         far_copy(k).wait_send()
-    for buf, axis, me, cnt, send, recv in (
-        (part_w, "wide", w, nw, pw_send, pw_recv), (part_n, "narrow", n, nn, pn_send, pn_recv)
-    ):
-        for k in range(1, cnt):
-            pltpu.make_async_remote_copy(
-                src_ref=buf.at[me], dst_ref=buf.at[me], send_sem=send.at[k - 1], recv_sem=recv.at[me],
-                device_id={axis: lax.rem(me + k, cnt)}, device_id_type=MESH,
-            ).wait_send()
+    gram_wide[2]()
+    gram_narrow[2]()
+    if direct:
+        last_both[2]()
+    else:
+        last_wide[2]()
+        last_narrow[2]()
 
 
 def solution(mesh):
@@ -356,12 +406,18 @@
                 pltpu.VMEM((nb + 1, nb * probes, bs), bf16),
                 pltpu.VMEM((nb * probes, bs), f32),
                 pltpu.VMEM((3 * basis, nb * bs), bf16),
-                pltpu.VMEM((nw, probes + basis, 128), f32),
-                pltpu.VMEM((nn, probes + basis, 128), f32),
+                pltpu.VMEM((nw, basis, 128), f32),
+                pltpu.VMEM((nn, basis, 128), f32),
+                pltpu.VMEM((nw, probes, 128), f32),
+                pltpu.VMEM((nn, probes, 128), f32),
+                pltpu.VMEM((nw * nn, probes, 128), f32),
                 dma((2,)), dma((2,)),
                 dma((nw - 1,)), dma((nw - 1,)),
                 dma((nw - 1,)), dma((nw,)),
                 dma((nn - 1,)), dma((nn,)),
+                dma((nw - 1,)), dma((nw,)),
+                dma((nn - 1,)), dma((nn,)),
+                dma((nw * nn - 1,)), dma((nw * nn,)),
             ],
             compiler_params=pltpu.CompilerParams(
                 collective_id=0, has_side_effects=True, vmem_limit_bytes=56 * 2**20

time: 28.9 us -> 26.4 us (0.913)
  Pallas kernels: 25.3 us -> 22.8 us
    pallas_call x1, Pallas kernels: 25.3 us -> 22.8 us  [shards(): pl.pallas_call(functools.partial(body, nw, nn), out_shape=(jax.ShapeDtype...]
where the time goes in v2:
time: 26.4 us; the launch traced here: 26.2 us
  Pallas kernels  22.8 us (86%)
  local copies, waits for them, and re-layouts  2.07 us (8%)
  between operations  1.29 us (5%)
    pallas_call x1, Pallas kernels, shards(): pl.pallas_call(functools.partial(body, nw, nn), out_shape=(jax.ShapeDtype...  22.8 us
    unnamed x4, local copies, waits for them, and re-layouts  2.07 us

profile of v2, /device:TPU:0, one launch (start us, length us, event | category | flops | bytes accessed | tf_op | source)
XLA Modules:
  0.0 26.2 jit_solution(4852484143841891099)
XLA Ops:
  1.3 22.8 %lanczos_step.1 = (f32[8,8,256]{2,1,0:T(8,128)}, f32[8,16]{1,0:T(8,128)}) custom-call(bf16[3,8,256]{2,1,0:T(8,128)(2,1)} %bitcast.3, f32[8,8,256]{2,1,0:T(8,128)} %probe_hbm.1, f32[8,8,256]{2,1,0:T(8,128)} %kept_hbm.1, s32[1,1,2,64]{3,2,1,0:T(2,128)} %bitcast.5, s32[1,1]{1,0:T(1,128)S(6)} %copy.11.counts_hbm, s32[1,1,4,6]{3,2,1,0:T(4,128)} %send_hbm.1, ...), custom_call_target="tpu_custom_call" | custom-call | tf_op jit(solution)/shard_map/lanczos_step/pallas_call | solution.py:382
  24.1 0.0 copy-start
  24.1 1.5 %copy.12 = f32[8,8,256]{2,1,0:T(8,128)} copy(f32[8,8,256]{2,1,0:T(8,128)} %get-tuple-element.8) | data formatting | bytes 131072
  25.6 0.0 copy-done
  25.6 0.6 %copy.13 = f32[16,8]{0,1:T(8,128)} copy(f32[16,8]{0,1:T(8,128)S(1)} %bitcast.4) | data formatting | bytes 1024
Async XLA Ops:
  24.1 1.5 %copy-start = (f32[8,16]{1,0:T(8,128)S(1)}, f32[8,16]{1,0:T(8,128)}, u32[]{:S(2)}) copy-start(f32[8,16]{1,0:T(8,128)} %get-tuple-element.5) | copy-start | bytes 1540
